TPU v7x, 32 devices: a whole 2x2x4 slice. The times are simulated.
32 devices in a mesh: section: 2 (over x), dp: 16 (over z, y, core).
Axes of the slice: x: 2, y: 2, z: 4, core: 2. Of those that a mesh axis runs over, the one named last changes fastest.
Arguments:
- inputs: bfloat16 [2, 32, 256, 512], P('section', 'dp'), may hold values from -6 to 6
- lengths: int32 [2, 32, 8], P(None, 'dp'), may hold values from 8 to 32, as said below
- cotangent: bfloat16 [32, 256, 512], P('dp'), may hold values from -6 to 6
- matrices: bfloat16 [2, 7168, 512], P('section')
- vectors: bfloat16 [2, 5632], P('section')
- master_matrices: float32 [2, 7168, 512], P('section', 'dp'), may hold values from -0.005859375 to 0.005859375
- master_vectors: float32 [2, 5632], P('section', 'dp'), may hold values from -0.005859375 to 0.005859375
- matrix_mean: float32 [2, 7168, 512], P('section', 'dp'), may hold values from -128 to 128
- matrix_square: float32 [2, 7168, 512], P('section', 'dp'), may hold values from 2 to 200
- vector_mean: float32 [2, 5632], P('section', 'dp'), may hold values from -128 to 128
- vector_square: float32 [2, 5632], P('section', 'dp'), may hold values from 2 to 200
- adam_step: int32 [1], replicated, may hold values from 3000 to 5000
Outputs:
- layer_outputs: bfloat16 [2, 32, 256, 512], P('section', 'dp')
- input_grads: float32 [2, 32, 256, 512], P('section', 'dp')
- matrix_grads: float32 [2, 7168, 512], P('section', 'dp')
- vector_grads: float32 [2, 5632], P('section', 'dp')
- matrix_change: float32 [2, 7168, 512], P('section', 'dp')
- vector_change: float32 [2, 5632], P('section', 'dp')
- matrix_mean_new: float32 [2, 7168, 512], P('section', 'dp')
- matrix_square_new: float32 [2, 7168, 512], P('section', 'dp')
- vector_mean_new: float32 [2, 5632], P('section', 'dp')
- vector_square_new: float32 [2, 5632], P('section', 'dp')
- matrices_new: bfloat16 [2, 7168, 512], P('section')
- vectors_new: bfloat16 [2, 5632], P('section')
Inputs may be any that keep to these rules, and one draw needn't show every extreme that they name: lengths[s, r, :] are the lengths of the 8 sentences packed in row r of the source (s = 0) and of the target (s = 1), sentence j of a target row translating sentence j of the source row; a row's total is at most 256, the rest is padding, and every row has one sentence of exactly 32 tokens.
All inputs are finite; a program needn't handle non-finite values.
Results may differ from a plain program's by a relative error of at most 0.025.
Values may be sent and summed in bfloat16 or wider, within the bound.
No kernel may reach another device: no remote copies, remote signals or barrier semaphores. Data moves between devices by JAX's collectives and lax.ppermute only.
A program may use at most 256 MiB of HBM per device.

v0:
```python
import jax
import jax.numpy as jnp
from jax import lax
from jax.sharding import PartitionSpec as P

HEADS = 8
MICRO = 2


MASK_FILL = -1e30
NORM_EPS = 1e-05
ADAM_EPS = 1e-09
WARMUP_STEPS = 4000.0


def passed_along(array, axis, by):
    devices = lax.axis_size(axis)
    pairs = [(i, i + by) for i in range(devices) if 0 <= i + by < devices]
    return lax.ppermute(array, axis, pairs)


def layer_norm(hidden, norm_gain, norm_shift):
    centre = hidden - jnp.mean(hidden, axis=-1, keepdims=True)
    spread = jnp.mean(centre * centre, axis=-1, keepdims=True)
    return centre * lax.rsqrt(spread + NORM_EPS) * norm_gain + norm_shift


def smooth_act(values):
    return jax.nn.gelu(values, approximate=False)


def matmul(first_op, second_op):
    return jnp.dot(first_op, second_op, preferred_element_type=jnp.float32)


def matmul_tn(first_op, second_op):
    return lax.dot_general(
        first_op, second_op, (((0,), (0,)), ((), ())), preferred_element_type=jnp.float32
    )


def matmul_nt(first_op, second_op):
    return lax.dot_general(
        first_op, second_op, (((1,), (1,)), ((), ())), preferred_element_type=jnp.float32
    )


def segment_ids(sent_lens, seq_len):
    sent_ends = jnp.cumsum(sent_lens, axis=-1)
    position = jnp.arange(seq_len, dtype=jnp.int32)
    return jnp.sum((position[None, :, None] >= sent_ends[:, None, :]).astype(jnp.int32), axis=-1)


def mask_of(query_ids, key_ids, pad_id, causal):
    same_sent = query_ids[:, :, None] == key_ids[:, None, :]
    if causal:
        position = jnp.arange(query_ids.shape[1], dtype=jnp.int32)
        same_sent = same_sent & (position[None, :, None] >= position[None, None, :])
    return same_sent | (query_ids == pad_id)[:, :, None]


def attend_forward(queries, key_vecs, values, allowed):
    score_scale = queries.shape[-1] ** (-0.5)
    scores = (
        jnp.einsum("rqhd,rkhd->rhqk", queries, key_vecs, preferred_element_type=jnp.float32)
        * score_scale
    )
    scores = jnp.where(allowed[:, None], scores, MASK_FILL)
    row_max = jnp.max(scores, axis=-1, keepdims=True)
    exp_scores = jnp.exp(scores - row_max)
    row_total = jnp.sum(exp_scores, axis=-1, keepdims=True)
    attn_probs = (exp_scores / row_total).astype(jnp.bfloat16)
    result = jnp.einsum("rhqk,rkhd->rqhd", attn_probs, values, preferred_element_type=jnp.float32)
    return (result, row_max + jnp.log(row_total))


def attend_backward(queries, key_vecs, values, allowed, logsum, grad_out):
    score_scale = queries.shape[-1] ** (-0.5)
    scores = (
        jnp.einsum("rqhd,rkhd->rhqk", queries, key_vecs, preferred_element_type=jnp.float32)
        * score_scale
    )
    scores = jnp.where(allowed[:, None], scores, MASK_FILL)
    attn_probs = jnp.exp(scores - logsum)
    grad_values = jnp.einsum(
        "rhqk,rqhd->rkhd",
        attn_probs.astype(jnp.bfloat16),
        grad_out,
        preferred_element_type=jnp.float32,
    )
    grad_probs = jnp.einsum("rqhd,rkhd->rhqk", grad_out, values, preferred_element_type=jnp.float32)
    inner = jnp.sum(attn_probs * grad_probs, axis=-1, keepdims=True)
    grad_scores = (attn_probs * (grad_probs - inner)).astype(jnp.bfloat16)
    grad_queries = (
        jnp.einsum("rhqk,rkhd->rqhd", grad_scores, key_vecs, preferred_element_type=jnp.float32)
        * score_scale
    )
    grad_keys = (
        jnp.einsum("rhqk,rqhd->rkhd", grad_scores, queries, preferred_element_type=jnp.float32)
        * score_scale
    )
    return (grad_queries, grad_keys, grad_values)


def unpack(weights, small_vecs):
    model_width = weights.shape[1]
    ffn_width = (weights.shape[0] - 6 * model_width) // 2
    attn_in = weights[: 3 * model_width].reshape(model_width, 3 * model_width)
    attn_out = weights[3 * model_width : 4 * model_width]
    cross_w = weights[4 * model_width : 6 * model_width].reshape(model_width, 2 * model_width)
    ffn_in = weights[6 * model_width : 6 * model_width + ffn_width].reshape(model_width, ffn_width)
    ffn_out = weights[6 * model_width + ffn_width :]
    bias_in = small_vecs[:ffn_width]
    row_params = small_vecs[ffn_width:].reshape(7, model_width)
    return (attn_in, attn_out, cross_w, ffn_in, ffn_out, bias_in, row_params)


def pack_grads(mat_list, vec_list):
    model_width = mat_list[1].shape[0]
    grad_mat = jnp.concatenate(
        [
            mat_list[0].reshape(-1, model_width),
            mat_list[1],
            mat_list[2].reshape(-1, model_width),
            mat_list[3].reshape(-1, model_width),
            mat_list[4],
        ],
        axis=0,
    )
    return (grad_mat, jnp.concatenate(vec_list, axis=0))


def self_forward(source, attn_in, attn_out, allowed, head_count):
    row_count, seq_len, model_width = source.shape
    flat_low = source.reshape(row_count * seq_len, model_width)
    packed = (
        matmul(flat_low, attn_in)
        .astype(jnp.bfloat16)
        .reshape(row_count, seq_len, 3, head_count, model_width // head_count)
    )
    queries, key_vecs, values = (packed[:, :, 0], packed[:, :, 1], packed[:, :, 2])
    mixed, logsum = attend_forward(queries, key_vecs, values, allowed)
    mixed_low = mixed.astype(jnp.bfloat16).reshape(row_count * seq_len, model_width)
    return (matmul(mixed_low, attn_out), (queries, key_vecs, values, logsum, mixed_low))


def self_backward(source, attn_in, attn_out, allowed, kept_att, grad_branch):
    queries, key_vecs, values, logsum, mixed_low = kept_att
    row_count, seq_len, model_width = source.shape
    grad_low = grad_branch.astype(jnp.bfloat16)
    grad_attn_out = matmul_tn(mixed_low, grad_low)
    grad_mixed = matmul_nt(grad_low, attn_out).astype(jnp.bfloat16).reshape(queries.shape)
    grad_q, grad_k, grad_v = attend_backward(queries, key_vecs, values, allowed, logsum, grad_mixed)
    grad_packed = (
        jnp.stack([grad_q, grad_k, grad_v], axis=2)
        .reshape(row_count * seq_len, 3 * model_width)
        .astype(jnp.bfloat16)
    )
    flat_low = source.reshape(row_count * seq_len, model_width)
    return (matmul_tn(flat_low, grad_packed), grad_attn_out, matmul_nt(grad_packed, attn_in))


def ffn_forward(normed, ffn_in, bias_in, ffn_out, bias_out):
    normed_low = normed.astype(jnp.bfloat16)
    pre_act = matmul(normed_low, ffn_in) + bias_in
    activated, act_back = jax.vjp(smooth_act, pre_act)
    act_low = activated.astype(jnp.bfloat16)
    return (matmul(act_low, ffn_out) + bias_out, (normed_low, act_back, act_low))


def ffn_backward(ffn_in, ffn_out, kept_ffn, grad_branch):
    normed_low, act_back, act_low = kept_ffn
    grad_low = grad_branch.astype(jnp.bfloat16)
    grad_ffn_out = matmul_tn(act_low, grad_low)
    grad_bias_out = jnp.sum(grad_low.astype(jnp.float32), axis=0)
    grad_pre = act_back(matmul_nt(grad_low, ffn_out))[0].astype(jnp.bfloat16)
    grad_bias_in = jnp.sum(grad_pre.astype(jnp.float32), axis=0)
    return (
        matmul_tn(normed_low, grad_pre),
        grad_bias_in,
        grad_ffn_out,
        grad_bias_out,
        matmul_nt(grad_pre, ffn_in),
    )


def encoder_run(params, source, src_ids, pad_id, head_count, grad_pairs):
    attn_in, attn_out, cross_w, ffn_in, ffn_out, bias_in, row_params = params
    row_count, seq_len, model_width = source.shape
    allowed = mask_of(src_ids, src_ids, pad_id, False)
    branch, kept_att = self_forward(source, attn_in, attn_out, allowed, head_count)
    flat_in = source.reshape(row_count * seq_len, model_width).astype(jnp.float32)
    normed_one, back_one = jax.vjp(layer_norm, flat_in + branch, row_params[1], row_params[2])
    branch_two, kept_ffn = ffn_forward(normed_one, ffn_in, bias_in, ffn_out, row_params[0])
    normed_two, back_two = jax.vjp(
        layer_norm, normed_one + branch_two, row_params[3], row_params[4]
    )
    memory, back_three = jax.vjp(layer_norm, normed_two, row_params[5], row_params[6])
    memory_low = memory.astype(jnp.bfloat16)
    if grad_pairs is None:
        mem_pairs = matmul(memory_low, cross_w).astype(jnp.bfloat16)
        return (
            mem_pairs.reshape(row_count, seq_len, 2 * model_width),
            memory_low.reshape(row_count, seq_len, model_width),
        )
    grad_low = grad_pairs.reshape(row_count * seq_len, 2 * model_width)
    grad_cross = matmul_tn(memory_low, grad_low)
    grad_two, gain_three, shift_three = back_three(matmul_nt(grad_low, cross_w))
    grad_sum_two, gain_two, shift_two = back_two(grad_two)
    grad_ffn_in, grad_bias_in, grad_ffn_out, grad_bias_out, grad_normed = ffn_backward(
        ffn_in, ffn_out, kept_ffn, grad_sum_two
    )
    grad_sum_one, gain_one, shift_one = back_one(grad_sum_two + grad_normed)
    grad_attn_in, grad_attn_out, grad_source = self_backward(
        source, attn_in, attn_out, allowed, kept_att, grad_sum_one
    )
    packed_grads = pack_grads(
        [grad_attn_in, grad_attn_out, grad_cross, grad_ffn_in, grad_ffn_out],
        [
            grad_bias_in,
            grad_bias_out,
            gain_one,
            shift_one,
            gain_two,
            shift_two,
            gain_three,
            shift_three,
        ],
    )
    return (packed_grads, (grad_sum_one + grad_source).reshape(row_count, seq_len, model_width))


def decoder_run(params, target, tgt_ids, src_ids, pad_id, head_count, mem_pairs, grad_top):
    attn_in, attn_out, cross_w, ffn_in, ffn_out, bias_in, row_params = params
    row_count, seq_len, model_width = target.shape
    head_dim = model_width // head_count
    allowed = mask_of(tgt_ids, tgt_ids, pad_id, True)
    cross_allowed = mask_of(tgt_ids, src_ids, pad_id, False)
    branch, kept_att = self_forward(target, attn_in, attn_out, allowed, head_count)
    flat_in = target.reshape(row_count * seq_len, model_width).astype(jnp.float32)
    normed_one, back_one = jax.vjp(layer_norm, flat_in + branch, row_params[1], row_params[2])
    normed_low = normed_one.astype(jnp.bfloat16)
    cross_query, cross_out = (cross_w[:, :model_width], cross_w[:, model_width:])
    queries = (
        matmul(normed_low, cross_query)
        .astype(jnp.bfloat16)
        .reshape(row_count, seq_len, head_count, head_dim)
    )
    memory_heads = mem_pairs.reshape(row_count, seq_len, 2, head_count, head_dim)
    key_vecs, values = (memory_heads[:, :, 0], memory_heads[:, :, 1])
    mixed, logsum = attend_forward(queries, key_vecs, values, cross_allowed)
    mixed_low = mixed.astype(jnp.bfloat16).reshape(row_count * seq_len, model_width)
    normed_two, back_two = jax.vjp(
        layer_norm, normed_one + matmul(mixed_low, cross_out), row_params[3], row_params[4]
    )
    branch_three, kept_ffn = ffn_forward(normed_two, ffn_in, bias_in, ffn_out, row_params[0])
    result_top, back_three = jax.vjp(
        layer_norm, normed_two + branch_three, row_params[5], row_params[6]
    )
    grad_sum_three, gain_three, shift_three = back_three(
        grad_top.reshape(row_count * seq_len, model_width)
    )
    grad_ffn_in, grad_bias_in, grad_ffn_out, grad_bias_out, grad_normed = ffn_backward(
        ffn_in, ffn_out, kept_ffn, grad_sum_three
    )
    grad_sum_two, gain_two, shift_two = back_two(grad_sum_three + grad_normed)
    grad_mix_low = grad_sum_two.astype(jnp.bfloat16)
    grad_cross_out = matmul_tn(mixed_low, grad_mix_low)
    grad_mixed = matmul_nt(grad_mix_low, cross_out).astype(jnp.bfloat16).reshape(queries.shape)
    grad_q, grad_k, grad_v = attend_backward(
        queries, key_vecs, values, cross_allowed, logsum, grad_mixed
    )
    grad_pairs = (
        jnp.stack([grad_k, grad_v], axis=2)
        .reshape(row_count, seq_len, 2 * model_width)
        .astype(jnp.bfloat16)
    )
    grad_q_low = grad_q.reshape(row_count * seq_len, model_width).astype(jnp.bfloat16)
    grad_cross_query = matmul_tn(normed_low, grad_q_low)
    grad_sum_one, gain_one, shift_one = back_one(grad_sum_two + matmul_nt(grad_q_low, cross_query))
    grad_attn_in, grad_attn_out, grad_target = self_backward(
        target, attn_in, attn_out, allowed, kept_att, grad_sum_one
    )
    grad_cross = jnp.concatenate([grad_cross_query, grad_cross_out], axis=1)
    packed_grads = pack_grads(
        [grad_attn_in, grad_attn_out, grad_cross, grad_ffn_in, grad_ffn_out],
        [
            grad_bias_in,
            grad_bias_out,
            gain_one,
            shift_one,
            gain_two,
            shift_two,
            gain_three,
            shift_three,
        ],
    )
    result_low = result_top.astype(jnp.bfloat16).reshape(row_count, seq_len, model_width)
    grad_input = (grad_sum_one + grad_target).reshape(row_count, seq_len, model_width)
    return (result_low, packed_grads, grad_input, grad_pairs)


def adam_update(grad, master, mean_old, square_old, step_now, model_width):
    mean_new = 0.9 * mean_old + 0.1 * grad
    square_new = 0.98 * square_old + 0.02 * grad * grad
    rate = model_width ** (-0.5) * jnp.minimum(
        lax.rsqrt(step_now), step_now * WARMUP_STEPS ** (-1.5)
    )
    fixed_mean = mean_new / (1.0 - jnp.power(0.9, step_now))
    fixed_square = square_new / (1.0 - jnp.power(0.98, step_now))
    change = -rate * fixed_mean / (jnp.sqrt(fixed_square) + ADAM_EPS)
    return (change, mean_new, square_new, master + change)


def body(
    inputs,
    lengths,
    cotangent,
    matrices,
    vectors,
    master_matrices,
    master_vectors,
    matrix_mean,
    matrix_square,
    vector_mean,
    vector_square,
    adam_step,
):
    section_id = lax.axis_index("section")
    row_count, seq_len, model_width = (inputs.shape[1], inputs.shape[2], inputs.shape[3])
    rows_mb = row_count // MICRO
    pad_id = lengths.shape[2]
    head_count = HEADS
    src_ids = segment_ids(lengths[0], seq_len)
    tgt_ids = segment_ids(lengths[1], seq_len)
    params = unpack(matrices[0], vectors[0].astype(jnp.float32))
    local_in = inputs[0]
    grad_top_all = (
        cotangent.astype(jnp.float32) * (tgt_ids < pad_id).astype(jnp.float32)[:, :, None]
    )
    zero_pairs = jnp.zeros((rows_mb, seq_len, 2 * model_width), jnp.bfloat16)
    zero_mat = jnp.zeros(matrices.shape[1:], jnp.float32)
    zero_vec = jnp.zeros(vectors.shape[1:], jnp.float32)
    recv_fwd = zero_pairs
    recv_back = zero_pairs
    outs_buf = jnp.zeros(inputs.shape[1:], jnp.bfloat16)
    dins_buf = jnp.zeros(inputs.shape[1:], jnp.float32)
    total_mat, total_vec = (zero_mat, zero_vec)
    for step_index in range(MICRO + 2):

        def encoder_turn(carried, step_index=step_index):
            outs_now, dins_now, from_next = (carried[0], carried[1], carried[3])
            send_pairs, grad_mat, grad_vec = (zero_pairs, zero_mat, zero_vec)
            if step_index < MICRO:
                picked = slice(step_index * rows_mb, (step_index + 1) * rows_mb)
                send_pairs, memory_low = encoder_run(
                    params, local_in[picked], src_ids[picked], pad_id, head_count, None
                )
                outs_now = outs_now.at[picked].set(memory_low)
            if step_index >= 2:
                picked = slice((step_index - 2) * rows_mb, (step_index - 1) * rows_mb)
                (grad_mat, grad_vec), grad_input = encoder_run(
                    params, local_in[picked], src_ids[picked], pad_id, head_count, from_next
                )
                dins_now = dins_now.at[picked].set(grad_input)
            return (send_pairs, zero_pairs, grad_mat, grad_vec, outs_now, dins_now)

        def decoder_turn(carried, step_index=step_index):
            outs_now, dins_now, from_prev = (carried[0], carried[1], carried[2])
            grad_pairs, grad_mat, grad_vec = (zero_pairs, zero_mat, zero_vec)
            if 1 <= step_index <= MICRO:
                picked = slice((step_index - 1) * rows_mb, step_index * rows_mb)
                result_low, (grad_mat, grad_vec), grad_input, grad_pairs = decoder_run(
                    params,
                    local_in[picked],
                    tgt_ids[picked],
                    src_ids[picked],
                    pad_id,
                    head_count,
                    from_prev,
                    grad_top_all[picked],
                )
                outs_now = outs_now.at[picked].set(result_low)
                dins_now = dins_now.at[picked].set(grad_input)
            return (zero_pairs, grad_pairs, grad_mat, grad_vec, outs_now, dins_now)

        send_pairs, send_grads, grad_mat, grad_vec, outs_buf, dins_buf = lax.cond(
            section_id == 0, encoder_turn, decoder_turn, (outs_buf, dins_buf, recv_fwd, recv_back)
        )
        if step_index < MICRO:
            recv_fwd = passed_along(send_pairs, "section", 1)
        if 1 <= step_index <= MICRO:
            recv_back = passed_along(send_grads, "section", -1)
        total_mat = total_mat + grad_mat
        total_vec = total_vec + grad_vec
    shard_mat, shard_vec = (
        lax.psum_scatter(total_mat, "dp", scatter_dimension=0, tiled=True),
        lax.psum_scatter(total_vec, "dp", scatter_dimension=0, tiled=True),
    )
    step_now = adam_step[0].astype(jnp.float32)
    change_m, mean_m, square_m, master_m = adam_update(
        shard_mat, master_matrices[0], matrix_mean[0], matrix_square[0], step_now, model_width
    )
    change_v, mean_v, square_v, master_v = adam_update(
        shard_vec, master_vectors[0], vector_mean[0], vector_square[0], step_now, model_width
    )
    new_mat, new_vec = (
        lax.all_gather(master_m.astype(jnp.bfloat16)[None], "dp", axis=1, tiled=True),
        lax.all_gather(master_v.astype(jnp.bfloat16)[None], "dp", axis=1, tiled=True),
    )
    return (
        outs_buf[None],
        dins_buf[None],
        shard_mat[None],
        shard_vec[None],
        change_m[None],
        change_v[None],
        mean_m[None],
        square_m[None],
        mean_v[None],
        square_v[None],
        new_mat,
        new_vec,
    )


def solution(mesh):
    return jax.shard_map(
        body,
        mesh=mesh,
        in_specs=(
            P("section", "dp", None, None),
            P(None, "dp", None),
            P("dp", None, None),
            P("section", None, None),
            P("section", None),
            P("section", "dp", None),
            P("section", "dp"),
            P("section", "dp", None),
            P("section", "dp", None),
            P("section", "dp"),
            P("section", "dp"),
            P(),
        ),
        out_specs=(
            P("section", "dp", None, None),
            P("section", "dp", None, None),
            P("section", "dp", None),
            P("section", "dp"),
            P("section", "dp", None),
            P("section", "dp"),
            P("section", "dp", None),
            P("section", "dp", None),
            P("section", "dp"),
            P("section", "dp"),
            P("section", None, None),
            P("section", None),
        ),
        check_vma=False,
    )
```

profile of v0, /device:TPU:0, one launch (start us, length us, event | category | flops | bytes accessed | tf_op | source)
XLA Modules:
  0.0 700.3 jit_solution(17376470925182129237)
XLA Ops:
  24.9 19.2 %conditional.4 = (bf16[1,256,1024]{2,1,0:T(8,128)(2,1)}, bf16[2,256,512]{2,1,0:T(8,128)(2,1)}) conditional(s32[]{:T(128)} %convert_element_type.516, () %tuple.74, (bf16[2,256,512]{2,1,0:T(8,128)(2,1)S(1)}, bf16[512,1536]{1,0:T(8,128)(2,1)S(1)}, s32[2,256]{1,0:T(2,128)S(1)}, bf16[512,512]{1,0:T(8,128)(2,1)S(1)}, f32[7,512]{1,0:T(8,128)S(1)}, ...), branch_computations={%region_4.5_spmd, %region_5.14_spmd} | conditional | flops 2127302144 | bytes 28108390 | solution.py:387
  32.8 8.2 %fusion.398 = (f32[256]{0:T(256)S(1)}, f32[256,512]{1,0:T(8,128)S(1)}) fusion(f32[512]{0:T(512)S(1)} %bitcast.867, bf16[2048,512]{1,0:T(8,128)(2,1)} %get-tuple-element.243, bf16[512,2048]{1,0:T(8,128)(2,1)} %get-tuple-element.241, f32[2048]{0:T(1024)S(1)} %get-tuple-element.242, f32[256,512]{1,0:T(8,128)} %copy-done.92, f32[512]{0:T(512)S(1)} %bitcast.868, ...), kind=kOutput, calls=%fused_computation.818 | convolution fusion | flops 1109917440 | bytes 5260288 | tf_op jit(solution)/shard_map/cond/branch_1_fun/dot_general | solution.py:33
  49.9 9.9 %collective-permute-done = bf16[1,256,1024]{1,2,0:T(8,128)(2,1)S(1)} collective-permute-done((bf16[1,256,1024]{1,2,0:T(8,128)(2,1)}, bf16[1,256,1024]{1,2,0:T(8,128)(2,1)S(1)}, u32[]{:S(2)}, u32[]{:S(2)}) %collective-permute-start) | collective-permute-done | bytes 524320 | tf_op jit(solution)/shard_map/ppermute | solution.py:19
  59.8 36.5 %conditional.5 = (bf16[1,256,1024]{2,1,0:T(8,128)(2,1)}, bf16[1,256,1024]{1,2,0:T(8,128)(2,1)}, f32[7168,512]{1,0:T(8,128)}, f32[5632]{0:T(1024)S(1)}, bf16[2,25...) conditional(s32[]{:T(128)} %convert_element_type.516, (bf16[2,256,512]{2,1,0:T(8,128)(2,1)S(1)}, ...), branch_computations={%region_14.41_spmd, %region_41.50_spmd} | conditional | flops 6522265600 | bytes 331898816 | solution.py:387
  76.1 8.2 %fusion.404 = (f32[256]{0:T(256)S(1)}, f32[256,512]{1,0:T(8,128)S(1)}) fusion(f32[512]{0:T(512)S(1)} %bitcast.870, bf16[2048,512]{1,0:T(8,128)(2,1)} %get-tuple-element.265, bf16[512,2048]{1,0:T(8,128)(2,1)} %get-tuple-element.263, f32[2048]{0:T(1024)S(1)} %get-tuple-element.264, f32[256,512]{1,0:T(8,128)} %copy-done.93, f32[512]{0:T(512)S(1)} %bitcast.871, ...), kind=kOutput, calls=%fused_computation.822 | convolution fusion | flops 1109917440 | bytes 5260288 | tf_op jit(solution)/shard_map/cond/branch_1_fun/dot_general | solution.py:33
  87.3 7.1 %broadcast_in_dim.262 = f32[7168,512]{1,0:T(8,128)} broadcast(f32[]{:T(128)} %constant.617.clone), dimensions={} | broadcast | bytes 14680068 | tf_op jit(solution)/shard_map/broadcast_in_dim | solution.py:342
  101.0 67.1 %collective-permute-start.1 = (bf16[1,256,1024]{1,2,0:T(8,128)(2,1)}, bf16[1,256,1024]{1,2,0:T(8,128)(2,1)}, u32[]{:S(2)}, u32[]{:S(2)}) collective-permute-start(bf16[1,256,1024]{1,2,0:T(8,128)(2,1)} %copy.235), channel_id=1, source_target_pairs={{0,16},{1,17},{2,18},{3,19},{4,20},{5,21},{6,22},{7,23},{8,24},{9,... | collective-permute-start | bytes 1572872 | tf_op jit(solution)/shard_map/ppermute | solution.py:19
  168.0 6.5 collective-permute-done.2
  178.8 88.3 %conditional.6 = (bf16[1,256,1024]{1,2,0:T(8,128)(2,1)}, f32[7168,512]{1,0:T(8,128)}, f32[5632]{0:T(1024)}, f32[2,256,512]{2,1,0:T(8,128)}, bf16[1,2,256,512]{3,2,1,0:T(8,128)(2,1)}) conditional(s32[]{:T(128)} %convert_element_type.516, (bf16[2,256,512]{2,1,0:T(8,128)(2,1)S(1)}, bf16[512,1536]{1,0:T(8,128)(2,1)S(1)}, s32[2,256]{1,0:T(2,128)S(1)}, ...), branch_computations={%region_50.77_spmd, %region_77.101_spmd} | conditional | flops 6522265600 | bytes 323460864 | solution.py:387
  194.1 5.1 multiply_convert_fusion.7
  221.3 4.6 reshape.2246
  243.1 5.2 reshape.2248
  248.3 4.7 constant_dynamic-update-slice_fusion.22
  269.6 38.6 %collective-permute-done.3 = bf16[1,256,1024]{2,1,0:T(8,128)(2,1)} collective-permute-done((bf16[1,256,1024]{2,1,0:T(8,128)(2,1)S(1)}, bf16[1,256,1024]{2,1,0:T(8,128)(2,1)}, u32[]{:S(2)}, u32[]{:S(2)}) %collective-permute-start.3) | collective-permute-done | bytes 524320 | tf_op jit(solution)/shard_map/ppermute | solution.py:19
  308.2 78.8 %conditional.7 = (f32[7168,512]{1,0:T(8,128)}, f32[5632]{0:T(1024)}, f32[2,256,512]{2,1,0:T(8,128)}) conditional(s32[]{:T(128)} %convert_element_type.516, f32[2,256,512]{2,1,0:T(8,128)} %get-tuple-element.340, (bf16[2,256,512]{2,1,0:T(8,128)(2,1)S(1)}, bf16[512,1536]{1,0:T(8,128)(2,1)S(1)}, s32[2,256]{1,0:T(2,128)S(1)}, ...), branch_computations={%region_101.102_spmd, %region_102.126_spmd} | conditional | flops 5840302080 | bytes 213900416 | solution.py:387
  315.0 5.1 multiply_convert_fusion.9
  342.0 4.6 reshape.2258
  363.8 5.2 reshape.2260
  369.0 4.8 constant_dynamic-update-slice_fusion.33
  387.1 21.0 %add_add_fusion.12 = f32[7168,512]{1,0:T(8,128)} fusion(f32[7168,512]{1,0:T(8,128)} %get-tuple-element.345, f32[7168,512]{1,0:T(8,128)} %get-tuple-element.343, f32[7168,512]{1,0:T(8,128)} %get-tuple-element.344), kind=kLoop, calls=%fused_computation.774 | loop fusion | flops 7340032 | bytes 58720256 | tf_op jit(solution)/shard_map/add | solution.py:394
  409.1 148.7 %reduce-scatter.2.cloned.1.call-done = f32[448,512]{1,0:T(8,128)} async-done(((f32[7168,512]{1,0:T(8,128)}), f32[448,512]{1,0:T(8,128)}) %reduce-scatter.2.cloned.1.call-update) | async-done | bytes 917520 | tf_op jit(solution)/shard_map/reduce_scatter | solution.py:397
  564.2 61.4 %all-reduce.3 = f32[5632]{0:T(1024)S(1)} all-reduce(f32[5632]{0:T(1024)S(1)} %add_add_fusion.13), channel_id=5, replica_groups=mesh['section'=2,'dp'=16] {'dp'}, use_global_device_ids=true, to_apply=%region_127.128.clone | all-reduce | flops 5632 | bytes 45056
  625.9 57.6 %all-reduce.2 = bf16[5632]{0:T(1024)(128)(2,1)S(1)} all-reduce(bf16[5632]{0:T(1024)(128)(2,1)S(1)} %dynamic-update-slice.25), channel_id=3, replica_groups=mesh['section'=2,'dp'=16] {'dp'}, use_global_device_ids=true, to_apply=%add.2 | all-reduce | flops 5632 | bytes 22528
  686.4 6.6 copy.351
  (338 shorter events, 185.1 us)
Async XLA Ops:
  7.2 550.6 %reduce-scatter.2.cloned.1.call-start = ((), (), s32[]{:S(2)}) async-start(), calls=%async_computation.1 | async-start | bytes 15597568 | tf_op jit(solution)/shard_map/reduce_scatter | solution.py:397
  17.1 42.7 %copy-start.131 = (f32[1,2048]{1,0:T(1,128)}, f32[1,2048]{1,0:T(1,128)S(1)}, u32[]{:S(2)}) copy-start(f32[1,2048]{1,0:T(1,128)S(1)} %slice_convert_fusion) | copy-start | bytes 24580
  20.0 4.9 copy-start.6
  46.2 13.7 %collective-permute-start = (bf16[1,256,1024]{1,2,0:T(8,128)(2,1)}, bf16[1,256,1024]{1,2,0:T(8,128)(2,1)S(1)}, u32[]{:S(2)}, u32[]{:S(2)}) collective-permute-start(bf16[1,256,1024]{1,2,0:T(8,128)(2,1)} %copy.234), channel_id=1, source_target_pairs={{0,16},{1,17},{2,18},{3,19},{4,20},{5,21},{6,22},{7,23},{8,24},{9,... | collective-permute-start | bytes 1572872 | tf_op jit(solution)/shard_map/ppermute | solution.py:19
  96.4 82.4 %copy-start.128 = (f32[5632]{0:T(1024)}, f32[5632]{0:T(1024)S(1)}, u32[]{:S(2)}) copy-start(f32[5632]{0:T(1024)S(1)} %get-tuple-element.346) | copy-start | bytes 67588
  97.6 76.9 %collective-permute-start.2 = (bf16[1,256,1024]{2,1,0:T(8,128)(2,1)S(1)}, bf16[1,256,1024]{2,1,0:T(8,128)(2,1)}, u32[]{:S(2)}, u32[]{:S(2)}) collective-permute-start(bf16[1,256,1024]{2,1,0:T(8,128)(2,1)S(1)} %copy.236), channel_id=1, source_target_pairs={{16,0},{17,1},{18,2},{19,3},{20,4},{21,5},{22,6},{23,7},{24,8},{25... | collective-permute-start | bytes 1572872 | tf_op jit(solution)/shard_map/ppermute | solution.py:19
  101.0 77.8 %collective-permute-start.1 = (bf16[1,256,1024]{1,2,0:T(8,128)(2,1)}, bf16[1,256,1024]{1,2,0:T(8,128)(2,1)}, u32[]{:S(2)}, u32[]{:S(2)}) collective-permute-start(bf16[1,256,1024]{1,2,0:T(8,128)(2,1)} %copy.235), channel_id=1, source_target_pairs={{0,16},{1,17},{2,18},{3,19},{4,20},{5,21},{6,22},{7,23},{8,24},{9,... | collective-permute-start | bytes 1572872 | tf_op jit(solution)/shard_map/ppermute | solution.py:19
  192.7 13.9 %copy-start.19 = (f32[256,512]{1,0:T(8,128)}, f32[256,512]{1,0:T(8,128)S(1)}, u32[]{:S(2)}) copy-start(f32[256,512]{1,0:T(8,128)S(1)} %get-tuple-element.522) | copy-start | bytes 1572868 | tf_op jit(solution)/shard_map/cond
  194.1 5.1 copy-start.96
  253.0 11.7 %copy-start.37 = (f32[256,512]{1,0:T(8,128)S(1)}, f32[256,512]{1,0:T(8,128)}, u32[]{:S(2)}) copy-start(f32[256,512]{1,0:T(8,128)} %copy-done.35) | copy-start | bytes 1572868 | tf_op jit(solution)/shard_map/cond
  253.0 11.7 %copy-start.53 = (bf16[1,256,3,8,64]{1,4,3,2,0:T(8,128)(2,1)S(1)}, bf16[1,256,3,8,64]{1,4,3,2,0:T(8,128)(2,1)}, u32[]{:S(2)}) copy-start(bf16[1,256,3,8,64]{1,4,3,2,0:T(8,128)(2,1)} %copy-done.52) | copy-start | bytes 2359300 | tf_op jit(solution)/shard_map/cond
  268.3 39.9 %collective-permute-start.3 = (bf16[1,256,1024]{2,1,0:T(8,128)(2,1)S(1)}, bf16[1,256,1024]{2,1,0:T(8,128)(2,1)}, u32[]{:S(2)}, u32[]{:S(2)}) collective-permute-start(bf16[1,256,1024]{2,1,0:T(8,128)(2,1)S(1)} %copy.237), channel_id=1, source_target_pairs={{16,0},{17,1},{18,2},{19,3},{20,4},{21,5},{22,6},{23,7},{24,8},{25... | collective-permute-start | bytes 1572872 | tf_op jit(solution)/shard_map/ppermute | solution.py:19
  313.5 13.7 %copy-start.21 = (f32[256,512]{1,0:T(8,128)}, f32[256,512]{1,0:T(8,128)S(1)}, u32[]{:S(2)}) copy-start(f32[256,512]{1,0:T(8,128)S(1)} %get-tuple-element.540) | copy-start | bytes 1572868 | tf_op jit(solution)/shard_map/cond
  315.0 5.1 copy-start.97
  369.0 4.8 copy-start.73
  373.8 11.6 %copy-start.55 = (bf16[1,256,3,8,64]{1,4,3,2,0:T(8,128)(2,1)S(1)}, bf16[1,256,3,8,64]{1,4,3,2,0:T(8,128)(2,1)}, u32[]{:S(2)}) copy-start(bf16[1,256,3,8,64]{1,4,3,2,0:T(8,128)(2,1)} %copy-done.54) | copy-start | bytes 2359300 | tf_op jit(solution)/shard_map/cond
  408.1 149.7 %copy-start.123 = (f32[1,448,512]{2,1,0:T(8,128)S(1)}, f32[1,448,512]{2,1,0:T(8,128)}, u32[]{:S(2)}) copy-start(f32[1,448,512]{2,1,0:T(8,128)} %param.41) | copy-start | bytes 2752516
  408.1 149.7 %copy-start.124 = (f32[1,448,512]{2,1,0:T(8,128)S(1)}, f32[1,448,512]{2,1,0:T(8,128)}, u32[]{:S(2)}) copy-start(f32[1,448,512]{2,1,0:T(8,128)} %param.44) | copy-start | bytes 2752516
  408.1 149.7 %copy-start.125 = (f32[1,448,512]{2,1,0:T(8,128)S(1)}, f32[1,448,512]{2,1,0:T(8,128)}, u32[]{:S(2)}) copy-start(f32[1,448,512]{2,1,0:T(8,128)} %param.43) | copy-start | bytes 2752516
  408.1 278.3 %all-gather.4.cloned.1.call-start = ((), (), s32[]{:S(2)}) async-start(), calls=%async_computation.2 | async-start | bytes 7798784 | tf_op jit(solution)/shard_map/all_gather | solution.py:408
  557.8 4.8 copy-start.147
  557.8 5.5 copy-start.145
  557.8 5.5 copy-start.146
  557.9 5.5 copy-start.129
  (44 other events, 89.8 us)
Sparse Core Ops, SparseCore 0:
  408.3 149.4 reduce-scatter.1
  561.5 68.2 all-gather.3
where the time goes:
time: 711 us; the launch traced here: 700 us
  waiting for transfers between devices  208 us (29%)
  local copies, waits for them, and re-layouts  136 us (19%)
  blocking collectives  119 us (17%)
  matrix products  92.3 us (13%)
  starting transfers between devices  71 us (10%)
  other arithmetic  38.6 us (5%)
  loops' own time  18.3 us (3%)
  between operations  16.9 us (2%)
    reduce_scatter x1, waiting for transfers between devices, body(): lax.psum_scatter(total_mat, 'dp', scatter_dimension=0, tiled=True)  149 us
    unnamed x2, blocking collectives  119 us
    ppermute x4, starting transfers between devices, passed_along(): return lax.ppermute(array, axis, pairs)  71 us
    ppermute x4, waiting for transfers between devices, passed_along(): return lax.ppermute(array, axis, pairs)  59.2 us
    cond x118, local copies, waits for them, and re-layouts  50.6 us
    dot_general x16, matrix products, matmul(): return jnp.dot(first_op, second_op, preferred_element_type=jnp.float32)  38.3 us
    dot_general x10, matrix products, matmul_tn(): lax.dot_general(first_op, second_op, (((0,), (0,)), ((), ())), preferred_...  24.5 us
    add x1, other arithmetic, body(): total_mat = total_mat + grad_mat  21 us
  transfers between devices with their start and end apart: 6, of which 5 were waited for; matrix products, arithmetic and copies ran while one was open for 1% of the time, Pallas kernels for 0%

commit v1 on v0

--- a/solution.py
+++ b/solution.py
@@ -4,7 +4,7 @@
 from jax.sharding import PartitionSpec as P
 
 HEADS = 8
-MICRO = 2
+MICRO = 1
 
 
 MASK_FILL = -1e30
@@ -393,10 +393,20 @@
             recv_back = passed_along(send_grads, "section", -1)
         total_mat = total_mat + grad_mat
         total_vec = total_vec + grad_vec
-    shard_mat, shard_vec = (
-        lax.psum_scatter(total_mat, "dp", scatter_dimension=0, tiled=True),
-        lax.psum_scatter(total_vec, "dp", scatter_dimension=0, tiled=True),
-    )
+    ranks = lax.axis_size("dp")
+    mat_share, vec_share = total_mat.shape[0] // ranks, total_vec.shape[0] // ranks
+    vec_rows = 16 * (-(-vec_share // (16 * model_width)))
+    vec_block = jnp.pad(
+        total_vec.reshape(ranks, vec_share), ((0, 0), (0, vec_rows * model_width - vec_share))
+    ).reshape(ranks, vec_rows, model_width)
+    blocks = jnp.concatenate(
+        [total_mat.reshape(ranks, mat_share, model_width), vec_block], axis=1
+    ).astype(jnp.bfloat16)
+    summed = lax.psum_scatter(
+        blocks.reshape(-1, model_width), "dp", scatter_dimension=0, tiled=True
+    ).astype(jnp.float32)
+    shard_mat = summed[:mat_share]
+    shard_vec = summed[mat_share:].reshape(-1)[:vec_share]
     step_now = adam_step[0].astype(jnp.float32)
     change_m, mean_m, square_m, master_m = adam_update(
         shard_mat, master_matrices[0], matrix_mean[0], matrix_square[0], step_now, model_width
@@ -404,10 +414,13 @@
     change_v, mean_v, square_v, master_v = adam_update(
         shard_vec, master_vectors[0], vector_mean[0], vector_square[0], step_now, model_width
     )
-    new_mat, new_vec = (
-        lax.all_gather(master_m.astype(jnp.bfloat16)[None], "dp", axis=1, tiled=True),
-        lax.all_gather(master_v.astype(jnp.bfloat16)[None], "dp", axis=1, tiled=True),
-    )
+    vec_tail = jnp.pad(master_v, (0, vec_rows * model_width - vec_share))
+    low_block = jnp.concatenate(
+        [master_m, vec_tail.reshape(vec_rows, model_width)], axis=0
+    ).astype(jnp.bfloat16)
+    gathered = lax.all_gather(low_block, "dp", axis=0, tiled=False)
+    new_mat = gathered[:, :mat_share].reshape(1, -1, model_width)
+    new_vec = gathered[:, mat_share:].reshape(ranks, -1)[:, :vec_share].reshape(1, -1)
     return (
         outs_buf[None],
         dins_buf[None],

time: 711 us -> 557 us (0.78); the launches traced: 700 us -> 555 us
  blocking collectives: 119 us -> 0 us
  waiting for transfers between devices: 208 us -> 313 us
  starting transfers between devices: 71 us -> 2.71 us
  local copies, waits for them, and re-layouts: 136 us -> 97 us
  matrix products: 92.3 us -> 74.2 us
    unnamed x2 -> x0, blocking collectives: 119 us -> none
    ppermute x4 -> x2, waiting for transfers between devices: 59.2 us -> 153 us  [passed_along(): return lax.ppermute(array, axis, pairs)]
    ppermute x4 -> x2, starting transfers between devices: 71 us -> 2.64 us  [passed_along(): return lax.ppermute(array, axis, pairs)]
    all_gather x1, waiting for transfers between devices: 0.01 us -> 67.5 us  [body(): gathered = lax.all_gather(low_block, 'dp', axis=0, tiled=False)]
    reduce_scatter x1, waiting for transfers between devices: 149 us -> 93.1 us  [body(): lax.psum_scatter(blocks.reshape(-1, model_width), 'dp', scatter_dimension...]
    cond x118 -> x86, local copies, waits for them, and re-layouts: 50.6 us -> 20.7 us
    add x2 -> x0, other arithmetic: 21.8 us -> none  [the longest x1 21 us: body(): total_mat = total_mat + grad_mat]
    reshape x0 -> x6, local copies, waits for them, and re-layouts: none -> 13.9 us  [the longest x2 9.03 us: self_forward(): packed = matmul(flat_low, attn_in).astype(jnp.bfloat16).reshape(row_count...]
  transfers between devices with their start and end apart: 6 -> 4, of which waited for: 5 -> 4; matrix products, arithmetic and copies ran while one was open for 1% -> 1% of each run, Pallas kernels for 0% -> 0%
where the time goes in v1:
time: 557 us; the launch traced here: 555 us
  waiting for transfers between devices  313 us (56%)
  local copies, waits for them, and re-layouts  97 us (17%)
  matrix products  74.2 us (13%)
  other arithmetic  38.6 us (7%)
  between operations  15.4 us (3%)
  loops' own time  13.8 us (2%)
    ppermute x2, waiting for transfers between devices, passed_along(): return lax.ppermute(array, axis, pairs)  153 us
    reduce_scatter x1, waiting for transfers between devices, body(): lax.psum_scatter(blocks.reshape(-1, model_width), 'dp', scatter_dimension...  93.1 us
    all_gather x1, waiting for transfers between devices, body(): gathered = lax.all_gather(low_block, 'dp', axis=0, tiled=False)  67.5 us
    dot_general x8, matrix products, matmul(): return jnp.dot(first_op, second_op, preferred_element_type=jnp.float32)  38 us
    cond x86, local copies, waits for them, and re-layouts  20.7 us
    another operation x3, loops' own time, body(): lax.cond(section_id == 0, encoder_turn, decoder_turn, (outs_buf, dins_buf...  13.8 us
    another operation x3, other arithmetic  13.5 us
    dot_general x5, matrix products, matmul_nt(): lax.dot_general(first_op, second_op, (((1,), (1,)), ((), ())), preferred_...  11.9 us
  transfers between devices with their start and end apart: 4, of which 4 were waited for; matrix products, arithmetic and copies ran while one was open for 1% of the time, Pallas kernels for 0%

profile of v1, /device:TPU:0, one launch (start us, length us, event | category | flops | bytes accessed | tf_op | source)
XLA Modules:
  0.0 555.1 jit_solution(15415377889889833300)
XLA Ops:
  12.6 4.6 slice_bitcast_fusion.6
  17.9 4.1 reshape.691
  22.0 4.4 reshape.693
  26.4 53.3 %conditional.3 = (bf16[2,256,1024]{2,1,0:T(8,128)(2,1)}, bf16[2,256,512]{2,1,0:T(8,128)(2,1)}) conditional(s32[]{:T(128)} %convert_element_type.288, () %tuple.74, (bf16[1,2,256,512]{3,2,1,0:T(8,128)(2,1)S(1)}, bf16[512,1536]{1,0:T(8,128)(2,1)}, s32[2,256]{1,0:T(2,128)S(1)}, bf16[512,512]{1,0:T(8,128)(2,1)S(1)}, f32[7,512]{1,0:T(8,128)S(1)}, ...), branch_computations={%region_4.5_spmd, %region_5.14_spmd} | conditional | flops 4116973824 | bytes 58094664 | solution.py:387
  26.4 3.5 convolution_convert_fusion
  30.1 5.1 reshape.717
  51.3 13.6 %fusion.195 = (f32[512]{0:T(512)S(1)}, f32[512,512]{1,0:T(8,128)S(1)}) fusion(f32[512]{0:T(512)S(1)} %bitcast.410, bf16[2048,512]{1,0:T(8,128)(2,1)} %get-tuple-element.207, bf16[512,2048]{1,0:T(8,128)(2,1)} %get-tuple-element.205, f32[2048]{0:T(1024)S(1)} %get-tuple-element.206, f32[512,512]{1,0:T(8,128)} %copy-done.41, f32[512]{0:T(512)S(1)} %bitcast.411, ...), kind=kOutput, calls=%fused_computation.395 | convolution fusion | flops 2219834880 | bytes 6311936 | tf_op jit(solution)/shard_map/cond/branch_1_fun/dot_general | solution.py:33
  84.8 22.1 %collective-permute-done = bf16[2,256,1024]{1,2,0:T(8,128)(2,1)S(1)} collective-permute-done((bf16[2,256,1024]{1,2,0:T(8,128)(2,1)}, bf16[2,256,1024]{1,2,0:T(8,128)(2,1)S(1)}, u32[]{:S(2)}, u32[]{:S(2)}) %collective-permute-start) | collective-permute-done | bytes 1048608 | tf_op jit(solution)/shard_map/ppermute | solution.py:19
  106.9 12.1 %conditional.4 = (bf16[2,256,1024]{1,2,0:T(8,128)(2,1)}, f32[7168,512]{1,0:T(8,128)}, f32[5632]{0:T(1024)S(1)}, bf16[1,2,256,512]{3,2,1,0:T(8,128)(2,1)}, f32[2,256,512]{2,1,0:T(8,128)}) conditional(s32[]{:T(128)} %convert_element_type.288, (bf16[1,2,256,512]{3,2,1,0:T(8,128)(2,1)S(1)}, bf16[512,1536]{1,0:T(8,128)(2,1)}, ...), branch_computations={%region_14.41_spmd.clone, %region_41.42_spmd} | conditional | flops 13044996096 | bytes 524122368 | solution.py:387
  111.9 7.1 %broadcast_in_dim.195 = f32[7168,512]{1,0:T(8,128)} broadcast(f32[]{:T(128)} %constant.474.clone), dimensions={} | broadcast | bytes 14680068 | tf_op jit(solution)/shard_map/broadcast_in_dim | solution.py:342
  121.9 130.6 %collective-permute-done.1 = bf16[2,256,1024]{2,1,0:T(8,128)(2,1)S(1)} collective-permute-done((bf16[2,256,1024]{2,1,0:T(8,128)(2,1)S(1)}, bf16[2,256,1024]{2,1,0:T(8,128)(2,1)S(1)}, u32[]{:S(2)}, u32[]{:S(2)}) %collective-permute-start.1) | collective-permute-done | bytes 1048608 | tf_op jit(solution)/shard_map/ppermute | solution.py:19
  252.4 97.0 %conditional.5 = (f32[7168,512]{1,0:T(8,128)}, f32[5632]{0:T(1024)S(1)}, f32[2,256,512]{2,1,0:T(8,128)S(1)}) conditional(s32[]{:T(128)} %convert_element_type.288, f32[2,256,512]{2,1,0:T(8,128)S(1)} %copy-done.82, (bf16[1,2,256,512]{3,2,1,0:T(8,128)(2,1)}, bf16[512,1536]{1,0:T(8,128)(2,1)}, s32[2,256]{1,0:T(2,128)S(1)}, ...), branch_computations={%region_42.43_spmd, %region_43.67_spmd} | conditional | flops 11681658880 | bytes 390014976 | solution.py:387
  253.6 3.7 convolution_convert_fusion.2
  257.3 4.0 reshape.718
  273.1 12.0 %multiply_convert_fusion.1 = (bf16[512,2048]{1,0:T(8,128)(2,1)S(1)}, f32[512,2048]{1,0:T(8,128)}, f32[512,2048]{1,0:T(8,128)}) fusion(f32[2048]{0:T(1024)S(1)} %get-tuple-element.230, bf16[512,2048]{1,0:T(8,128)(2,1)S(1)} %copy-done.59, f32[512,512]{1,0:T(8,128)S(1)} %get-tuple-element.373, f32[512]{0:T(512)S(1)} %bitcast.370, f32[512]{0:T(512)S(1)} %bitcast.360, ...), kind=kOutput, calls=%fused_computation.98 | convolution fusion | flops 1144258560 | bytes 13647872 | tf_op jit(solution)/shard_map/cond/branch_1_fun/dot_general | solution.py:33
  295.6 5.8 %convert_reduce_fusion = (f32[2048]{0:T(1024)S(1)}, bf16[512,2048]{1,0:T(8,128)(2,1)S(1)}) fusion(f32[512,2048]{1,0:T(8,128)} %get-tuple-element.323, f32[512,2048]{1,0:T(8,128)} %get-tuple-element.374, f32[2048]{0:T(1024)S(1)} %get-tuple-element.230, bf16[512,512]{1,0:T(8,128)(2,1)S(1)} %get-tuple-element.313, bf16[2048,512]{1,0:T(8,128)(2,1)} %get-tuple-element.231), kind=kOutput, calls=%fused_computation.94 | convolution fusion | flops 1091565568 | bytes 13123584 | tf_op jit(solution)/shard_map/cond/branch_1_fun/dot_general | solution.py:43
  309.1 3.9 fusion.81
  313.0 3.5 fusion.106
  316.5 5.7 %reshape.680 = f32[2048,512]{1,0:T(8,128)} reshape(f32[512,2048]{1,0:T(8,128)} %fusion.106) | data formatting | bytes 8388608 | tf_op jit(solution)/shard_map/cond/branch_1_fun/reshape | solution.py:125
  349.7 13.5 %add_convert_fusion.17 = bf16[7168,512]{1,0:T(8,128)(2,1)} fusion(f32[7168,512]{1,0:T(8,128)} %get-tuple-element.260, f32[7168,512]{1,0:T(8,128)} %get-tuple-element.261), kind=kLoop, calls=%fused_computation.352 | loop fusion | flops 7340032 | bytes 36700160 | tf_op jit(solution)/shard_map/convert.23
  363.2 6.8 %pad_maximum_fusion.2 = bf16[16,464,512]{2,1,0:T(8,128)(2,1)} fusion(bf16[16,16,512]{2,1,0:T(8,128)(2,1)S(1)} %bitcast.350, bf16[16,448,512]{2,1,0:T(8,128)(2,1)} %bitcast.313), kind=kLoop, calls=%fused_computation.353 | loop fusion | flops 15204352 | bytes 15204352 | tf_op jit(solution)/shard_map/concatenate | solution.py:402
  371.1 93.1 %reduce-scatter.2.cloned.1.call-done = bf16[464,512]{1,0:T(8,128)(2,1)} async-done(((bf16[7424,512]{1,0:T(8,128)(2,1)}), bf16[464,512]{1,0:T(8,128)(2,1)}) %reduce-scatter.2.cloned.1.call-update) | async-done | bytes 475152 | tf_op jit(solution)/shard_map/reduce_scatter | solution.py:405
  471.9 67.5 %all-gather.2.cloned.1.call-done = bf16[16,464,512]{2,1,0:T(8,128)(2,1)} async-done(((bf16[1,464,512]{2,1,0:T(8,128)(2,1)}), bf16[16,464,512]{2,1,0:T(8,128)(2,1)}) %all-gather.2.cloned.1.call-update) | async-done | bytes 7602192 | tf_op jit(solution)/shard_map/all_gather | solution.py:421
  541.3 6.8 %slice.320 = bf16[16,448,512]{2,1,0:T(8,128)(2,1)} slice(bf16[16,464,512]{2,1,0:T(8,128)(2,1)} %all-gather.2.cloned.1.call-done), slice={[0:16], [0:448], [0:512]} | slice | bytes 14680064 | tf_op jit(solution)/shard_map/slice | solution.py:422
  (228 shorter events, 104.7 us)
Async XLA Ops:
  7.2 457.1 %reduce-scatter.2.cloned.1.call-start = ((), (), s32[]{:S(2)}) async-start(), calls=%async_computation.1 | async-start | bytes 8077312 | tf_op jit(solution)/shard_map/reduce_scatter | solution.py:405
  9.8 97.1 %copy-start.6 = (bf16[512,512]{1,0:T(8,128)(2,1)}, bf16[512,512]{1,0:T(8,128)(2,1)S(1)}, u32[]{:S(2)}) copy-start(bf16[512,512]{1,0:T(8,128)(2,1)S(1)} %slice_bitcast_fusion.8) | copy-start | bytes 1572868
  12.6 4.6 copy-start.76
  12.6 4.9 slice-start
  17.9 89.0 %copy-start.35 = (bf16[512,1024]{1,0:T(8,128)(2,1)}, bf16[512,1024]{1,0:T(8,128)(2,1)S(1)}, u32[]{:S(2)}) copy-start(bf16[512,1024]{1,0:T(8,128)(2,1)S(1)} %reshape.692) | copy-start | bytes 3145732
  17.9 8.5 %copy-start.10 = (bf16[1,2,256,512]{3,2,1,0:T(8,128)(2,1)S(1)}, bf16[1,2,256,512]{3,2,1,0:T(8,128)(2,1)}, u32[]{:S(2)}) copy-start(bf16[1,2,256,512]{3,2,1,0:T(8,128)(2,1)} %param.34) | copy-start | bytes 1572868
  82.0 24.9 %collective-permute-start = (bf16[2,256,1024]{1,2,0:T(8,128)(2,1)}, bf16[2,256,1024]{1,2,0:T(8,128)(2,1)S(1)}, u32[]{:S(2)}, u32[]{:S(2)}) collective-permute-start(bf16[2,256,1024]{1,2,0:T(8,128)(2,1)} %copy.208), channel_id=1, source_target_pairs={{0,16},{1,17},{2,18},{3,19},{4,20},{5,21},{6,22},{7,23},{8,24},{9,... | collective-permute-start | bytes 3145736 | tf_op jit(solution)/shard_map/ppermute | solution.py:19
  119.0 133.4 %copy-start.82 = (f32[2,256,512]{2,1,0:T(8,128)S(1)}, f32[2,256,512]{2,1,0:T(8,128)}, u32[]{:S(2)}) copy-start(f32[2,256,512]{2,1,0:T(8,128)} %get-tuple-element.257) | copy-start | bytes 3145732
  120.6 131.9 %collective-permute-start.1 = (bf16[2,256,1024]{2,1,0:T(8,128)(2,1)S(1)}, bf16[2,256,1024]{2,1,0:T(8,128)(2,1)S(1)}, u32[]{:S(2)}, u32[]{:S(2)}) collective-permute-start(bf16[2,256,1024]{2,1,0:T(8,128)(2,1)S(1)} %copy.209), channel_id=1, source_target_pairs={{16,0},{17,1},{18,2},{19,3},{20,4},{21,5},{22,6},{23,7},{24,8},{25... | collective-permute-start | bytes 3145736 | tf_op jit(solution)/shard_map/ppermute | solution.py:19
  264.9 5.1 copy-start.54
  273.1 12.0 %copy-start.64 = (bf16[2048,512]{1,0:T(8,128)(2,1)S(1)}, bf16[2048,512]{1,0:T(8,128)(2,1)}, u32[]{:S(2)}) copy-start(bf16[2048,512]{1,0:T(8,128)(2,1)} %get-tuple-element.231) | copy-start | bytes 6291460 | tf_op jit(solution)/shard_map/cond
  295.6 5.9 %copy-start.56 = (bf16[512,512]{1,0:T(8,128)(2,1)}, bf16[512,512]{1,0:T(8,128)(2,1)S(1)}, u32[]{:S(2)}) copy-start(bf16[512,512]{1,0:T(8,128)(2,1)S(1)} %get-tuple-element.313) | copy-start | bytes 1572868 | tf_op jit(solution)/shard_map/cond
  295.6 5.9 %copy-start.60 = (bf16[512,2048]{1,0:T(8,128)(2,1)S(1)}, bf16[512,2048]{1,0:T(8,128)(2,1)}, u32[]{:S(2)}) copy-start(bf16[512,2048]{1,0:T(8,128)(2,1)} %get-tuple-element.229) | copy-start | bytes 6291460 | tf_op jit(solution)/shard_map/cond
  303.2 5.8 %copy-start.74 = (f32[5632]{0:T(1024)}, f32[5632]{0:T(1024)S(1)}, u32[]{:S(2)}) copy-start(f32[5632]{0:T(1024)S(1)} %constant_dynamic-update-slice_fusion.4) | copy-start | bytes 67588 | tf_op jit(solution)/shard_map/cond
  303.7 26.4 %copy-start.17 = (f32[512,512]{1,0:T(8,128)}, f32[512,512]{1,0:T(8,128)S(1)}, u32[]{:S(2)}) copy-start(f32[512,512]{1,0:T(8,128)S(1)} %get-tuple-element.317) | copy-start | bytes 3145732 | tf_op jit(solution)/shard_map/cond
  309.1 3.9 copy-start.66
  316.5 5.7 %copy-start.55 = (bf16[2,256,1,8,64]{1,4,3,0,2:T(8,128)(2,1)S(1)}, bf16[2,256,1,8,64]{1,4,3,0,2:T(8,128)(2,1)}, u32[]{:S(2)}) copy-start(bf16[2,256,1,8,64]{1,4,3,0,2:T(8,128)(2,1)} %copy-done.54) | copy-start | bytes 1572868 | tf_op jit(solution)/shard_map/cond
  322.1 3.4 copy-start.3
  338.4 3.5 copy-start.21
  346.0 3.3 copy-start.83
  349.5 13.7 %copy-start.84 = (f32[2,256,512]{2,1,0:T(8,128)}, f32[2,256,512]{2,1,0:T(8,128)S(1)}, u32[]{:S(2)}) copy-start(f32[2,256,512]{2,1,0:T(8,128)S(1)} %get-tuple-element.259) | copy-start | bytes 3145732
  370.1 95.4 %copy-start.71 = (f32[1,448,512]{2,1,0:T(8,128)S(1)}, f32[1,448,512]{2,1,0:T(8,128)}, u32[]{:S(2)}) copy-start(f32[1,448,512]{2,1,0:T(8,128)} %param.39) | copy-start | bytes 2752516
  370.1 95.4 %copy-start.72 = (f32[1,448,512]{2,1,0:T(8,128)S(1)}, f32[1,448,512]{2,1,0:T(8,128)}, u32[]{:S(2)}) copy-start(f32[1,448,512]{2,1,0:T(8,128)} %param.42) | copy-start | bytes 2752516
  370.1 169.3 %all-gather.2.cloned.1.call-start = ((), (), s32[]{:S(2)}) async-start(), calls=%async_computation.2 | async-start | bytes 8077312 | tf_op jit(solution)/shard_map/all_gather | solution.py:421
  (26 other events, 47.3 us)
Sparse Core Ops, SparseCore 0:
  370.2 93.9 reduce-scatter.1
  469.8 69.5 all-gather.1
